TPU v7x, 32 devices: a whole 2x2x4 slice. The times are simulated.
32 devices in a mesh: ctx: 8 (over z, x), head: 4 (over y, core).
Axes of the slice: x: 2, y: 2, z: 4, core: 2. Of those that a mesh axis runs over, the one named last changes fastest.
Arguments:
- queries: bfloat16 [8192, 4096], P('ctx', 'head'), may hold values from -104 to 104
- cache_keys: bfloat16 [3072, 4096], P('ctx', 'head'), may hold values from -4 to 4
- cache_values: bfloat16 [3072, 4096], P('ctx', 'head'), may hold values from -6 to 6
- reflect: bfloat16 [8, 32, 64, 128], P('ctx', 'head'), may hold values from -6 to 6
- betas: bfloat16 [8, 32, 64], P('ctx', 'head'), may hold values from 0.099609375 to 1.8984375
- chain_len: int32 [8], P('ctx'), may hold values from 4 to 8, as said below
- block_start: int32 [8, 4], P('ctx'), may hold values from 0 to 128
- live_len: int32 [8], P('ctx'), may hold values from 1 to 384
- w_out: bfloat16 [4096, 4096], P('head'), may hold values from -0.75 to 0.75
Outputs:
- projected: bfloat16 [8192, 4096], P('ctx', 'head')
Inputs may be any that keep to these rules, and one draw needn't show every extreme that they name: `chain_len`: every draw holds a request with 8 shards and one with 4.
All inputs are finite; a program needn't handle non-finite values.
Results may differ from a plain program's by a relative error of at most 0.012.
Values may be sent and summed in bfloat16 or wider, within the bound.
A program may use at most 128 MiB of HBM per device.

v0:
```python
import jax
import jax.numpy as jnp
from jax import lax
from jax.sharding import PartitionSpec as P

NQB = 4


def shifted(value, axis, steps):
    count = lax.axis_size(axis)
    pairs = [(source, (source + steps) % count) for source in range(count)]
    return lax.ppermute(value, axis, pairs)


def shard_product(factors, strengths):
    unit_rows = factors[0].astype(jnp.float32)
    unit_rows = unit_rows / jnp.sqrt(jnp.sum(unit_rows * unit_rows, axis=-1, keepdims=True) + 1e-06)
    rates = strengths[0].astype(jnp.float32)
    head_count = unit_rows.shape[0]
    head_size = unit_rows.shape[2]
    initial = jnp.broadcast_to(
        jnp.eye(head_size, dtype=jnp.float32), (head_count, head_size, head_size)
    )

    def reflect_once(product, column):
        vector = lax.dynamic_index_in_dim(unit_rows, column, 1, keepdims=False)
        weight = lax.dynamic_index_in_dim(rates, column, 1, keepdims=False)
        applied = jnp.einsum("hij,hj->hi", product, vector, precision=lax.Precision.HIGHEST)
        return (product - weight[:, None, None] * applied[:, :, None] * vector[:, None, :], None)

    product, unused = lax.scan(reflect_once, initial, jnp.arange(unit_rows.shape[1]))
    return product


def turn_rows(carried, product):
    return jnp.einsum("rhd,hde->rhe", carried, product, precision=lax.Precision.HIGHEST)


def attend(carried, shard_keys, shard_values, allowed):
    row_count, head_count, head_size = carried.shape
    key_layout = shard_keys.reshape(shard_keys.shape[0], head_count, head_size)
    value_layout = shard_values.reshape(shard_values.shape[0], head_count, head_size)
    scores = jnp.einsum(
        "rhd,khd->hrk", carried.astype(jnp.bfloat16), key_layout, preferred_element_type=jnp.float32
    ) * head_size ** (-0.5)
    scores = jnp.where(allowed[None], scores, -jnp.inf)
    block_top = jnp.max(scores, axis=-1)
    weights = jnp.exp(scores - block_top[..., None]).astype(jnp.bfloat16)
    block_total = jnp.sum(weights, axis=-1, dtype=jnp.float32)
    block_sum = jnp.einsum(
        "hrk,khd->rhd", weights, value_layout, preferred_element_type=jnp.float32
    )
    return (block_top, block_total, block_sum)


def merge_block(merged, block):
    row_top, row_total, summed = merged
    block_top, block_total, block_sum = block
    new_top = jnp.maximum(row_top, block_top)
    old_factor = jnp.exp(row_top - new_top)
    new_factor = jnp.exp(block_top - new_top)
    return (
        new_top,
        row_total * old_factor + new_factor * block_total,
        summed * old_factor.T[:, :, None] + new_factor.T[:, :, None] * block_sum,
    )


def shards(
    queries, cache_keys, cache_values, reflect, betas, chain_len, block_start, live_len, w_out
):
    row_count = queries.shape[0]
    head_count = reflect.shape[1]
    head_size = reflect.shape[3]
    shard_len = cache_keys.shape[0]
    block_rows = row_count // NQB
    carried = queries.reshape(row_count, head_count, head_size).astype(jnp.float32)
    positions = (
        block_start[0][:, None] + jnp.arange(block_rows, dtype=jnp.int32)[None, :]
    ).reshape(row_count)
    key_index = jnp.arange(shard_len, dtype=jnp.int32)
    length = chain_len[0]
    live_count = live_len[0]
    initial = (
        jnp.full((head_count, row_count), -jnp.inf, jnp.float32),
        jnp.zeros((head_count, row_count), jnp.float32),
        jnp.zeros((row_count, head_count, head_size), jnp.float32),
    )
    merged = merge_block(
        initial, attend(carried, cache_keys, cache_values, key_index[None, :] <= positions[:, None])
    )
    longest_chain = min(9, lax.axis_size("ctx"))
    own_shard = (cache_keys, cache_values, reflect, betas)
    arrived = own_shard
    for distance in range(1, longest_chain):
        previous = arrived
        arrived = shifted((arrived[0], arrived[1], arrived[2], arrived[3]), "ctx", 1)
        allowed = jnp.where(distance == length - 1, key_index >= shard_len - live_count, True)[
            None, :
        ]

        def visit(operands):
            carried_now, merged_now = operands
            turned = turn_rows(carried_now, shard_product(previous[2], previous[3]))
            return (
                turned,
                merge_block(merged_now, attend(turned, arrived[0], arrived[1], allowed)),
            )

        def unchanged(operands):
            return operands

        carried, merged = lax.cond(distance < length, visit, unchanged, (carried, merged))
    row_top, row_total, summed = merged
    attended = (
        (summed / row_total.T[:, :, None])
        .reshape(row_count, head_count * head_size)
        .astype(jnp.bfloat16)
    )
    partial_terms = jnp.dot(attended, w_out, preferred_element_type=jnp.float32)
    return lax.psum_scatter(
        partial_terms.astype(jnp.bfloat16), "head", scatter_dimension=1, tiled=True
    )


def solution(mesh):
    return jax.shard_map(
        shards,
        mesh=mesh,
        in_specs=(
            P("ctx", "head"),
            P("ctx", "head"),
            P("ctx", "head"),
            P("ctx", "head", None, None),
            P("ctx", "head", None),
            P("ctx"),
            P("ctx", None),
            P("ctx"),
            P("head", None),
        ),
        out_specs=P("ctx", "head"),
        check_vma=False,
    )
```

profile of v0, /device:TPU:0, one launch (start us, length us, event | category | flops | bytes accessed | tf_op | source)
XLA Modules:
  0.0 2291.5 jit_solution(18082597789125827502)
XLA Ops:
  6.5 2.9 collective-permute-start
  11.0 20.1 collective-permute-done
  31.1 16.8 collective-permute-done.1
  48.0 16.9 collective-permute-done.4
  64.9 16.8 collective-permute-done.5
  86.3 2.9 copy.90
  89.9 8.6 collective-permute-done.8
  98.5 17.0 collective-permute-done.9
  115.7 3.5 fusion.87
  119.2 16.2 collective-permute-done.12
  135.5 16.8 collective-permute-done.13
  152.3 2.6 convert_reduce_fusion.7
  156.5 12.5 collective-permute-done.16
  169.1 17.0 collective-permute-done.17
  186.0 8.2 fusion.88
  195.8 9.9 collective-permute-done.20
  205.7 16.8 collective-permute-done.21
  227.9 33.0 %collective-permute-done.14 = bf16[1,8,64,128]{3,1,2,0:T(8,128)(2,1)S(1)} collective-permute-done((bf16[1,8,64,128]{3,1,2,0:T(8,128)(2,1)S(1)}, bf16[1,8,64,128]{3,1,2,0:T(8,128)(2,1)S(1)}, u32[]{:S(2)}, u32[]{:S(2)}) %collective-permute-start.14) | collective-permute-done | bytes 131104 | tf_op jit(solution)/shard_map/ppermute | solution.py:12
  262.2 6.6 collective-permute-done.7
  268.8 6.4 collective-permute-done.11
  275.2 6.4 collective-permute-done.15
  281.7 6.5 collective-permute-done.19
  288.2 283.6 %conditional.7 = ((f32[1024,8,128]{0,2,1:T(8,128)}, f32[8,1024]{1,0:T(8,128)S(1)}, f32[8,1024]{1,0:T(8,128)S(1)}, f32[1024,8,128]{2,0,1:T(8,128)})) conditional(s32[]{:T(128)} %bitcast.104, (f32[1024,8,128]{0,2,1:T(8,128)}, f32[8,1024]{1,0:T(8,128)S(1)}, f32[8,1024]{1,0:T(8,128)S(1)}, f32[1024,8,128]{2,0,1:T(8,128)}) %tuple.77, ...), branch_computations={%region_2.3_spmd, %region_3.9_spmd} | conditional | flops 3268552192 | bytes 129260416 | solution.py:113
  288.9 261.7 %while.63 = (s32[]{:T(128)}, f32[8,128,128]{2,1,0:T(8,128)S(1)}, s32[64]{0:T(128)S(1)}, f32[8,64]{0,1:T(8,128)S(1)}, f32[8,64,128]{2,0,1:T(8,128)S(1)}, /*index=5*/s32[]{:T(128)}, s32[]{:T(128)}, s32[]{:T(128)}) while((s32[]{:T(128)}, f32[8,128,128]{2,1,0:T(8,128)S(1)}, s32[64]{0:T(128)S(1)}, f32[8,64]{0,1:T(8,128)S(1)}, ...), condition=%wide.region_6.6_spmd, body=%wide.region_5.5_spmd.sunk | while | flops 1836037 | bytes 1614071 | solution.py:31
  552.8 4.1 convolution_bitcast_fusion
  559.0 3.1 convert_reduce_fusion
  562.1 7.2 fusion.1
  571.8 286.6 %conditional.8 = ((f32[1024,8,128]{0,2,1:T(8,128)}, f32[8,1024]{1,0:T(8,128)S(1)}, f32[8,1024]{1,0:T(8,128)S(1)}, f32[1024,8,128]{2,0,1:T(8,128)})) conditional(s32[]{:T(128)} %bitcast.103, (f32[1024,8,128]{0,2,1:T(8,128)}, f32[8,1024]{1,0:T(8,128)S(1)}, f32[8,1024]{1,0:T(8,128)S(1)}, f32[1024,8,128]{2,0,1:T(8,128)}) %get-tuple-element.1201, ...), branch_computations={%region_9.10_spmd, %region_10.16_spmd} | conditional | flops 3268552192 | bytes 122966848 | solution.py:113
  572.2 262.6 %while.64 = (s32[]{:T(128)}, f32[8,128,128]{2,1,0:T(8,128)S(1)}, s32[64]{0:T(128)S(1)}, f32[8,64]{0,1:T(8,128)S(1)}, f32[8,64,128]{2,0,1:T(8,128)S(1)}, /*index=5*/s32[]{:T(128)}, s32[]{:T(128)}, s32[]{:T(128)}) while((s32[]{:T(128)}, f32[8,128,128]{2,1,0:T(8,128)S(1)}, s32[64]{0:T(128)S(1)}, f32[8,64]{0,1:T(8,128)S(1)}, ...), condition=%wide.region_13.13_spmd, body=%wide.region_12.12_spmd.sunk | while | flops 1836037 | bytes 1614071 | solution.py:31
  837.0 4.1 convolution_bitcast_fusion.1
  841.2 3.6 fusion.12
  844.8 3.0 convert_reduce_fusion.1
  847.9 8.4 fusion.13
  858.4 254.7 %conditional.9 = ((f32[1024,8,128]{0,2,1:T(8,128)}, f32[8,1024]{1,0:T(8,128)S(1)}, f32[8,1024]{1,0:T(8,128)S(1)}, f32[1024,8,128]{2,0,1:T(8,128)})) conditional(s32[]{:T(128)} %bitcast.102, (f32[1024,8,128]{0,2,1:T(8,128)}, f32[8,1024]{1,0:T(8,128)S(1)}, f32[8,1024]{1,0:T(8,128)S(1)}, f32[1024,8,128]{2,0,1:T(8,128)}) %get-tuple-element.1202, ...), branch_computations={%region_16.17_spmd, %region_17.23_spmd} | conditional | flops 3268552192 | bytes 122966848 | solution.py:113
  858.9 232.1 %while.65 = (s32[]{:T(128)}, f32[8,128,128]{2,1,0:T(8,128)S(1)}, s32[64]{0:T(128)S(1)}, f32[8,64]{0,1:T(8,128)S(1)}, f32[8,64,128]{2,0,1:T(8,128)S(1)}, /*index=5*/s32[]{:T(128)}, s32[]{:T(128)}, s32[]{:T(128)}) while((s32[]{:T(128)}, f32[8,128,128]{2,1,0:T(8,128)S(1)}, s32[64]{0:T(128)S(1)}, f32[8,64]{0,1:T(8,128)S(1)}, ...), condition=%wide.region_20.20_spmd, body=%wide.region_19.19_spmd.sunk | while | flops 1836037 | bytes 1614071 | solution.py:31
  1093.2 4.1 convolution_bitcast_fusion.2
  1099.3 3.1 convert_reduce_fusion.2
  1102.5 8.4 fusion.25
  1113.1 271.9 %conditional.10 = ((f32[1024,8,128]{0,2,1:T(8,128)}, f32[8,1024]{1,0:T(8,128)S(1)}, f32[8,1024]{1,0:T(8,128)S(1)}, f32[1024,8,128]{2,0,1:T(8,128)})) conditional(s32[]{:T(128)} %bitcast.101, (f32[1024,8,128]{0,2,1:T(8,128)}, f32[8,1024]{1,0:T(8,128)S(1)}, f32[8,1024]{1,0:T(8,128)S(1)}, f32[1024,8,128]{2,0,1:T(8,128)}) %get-tuple-element.1203, ...), branch_computations={%region_23.24_spmd, %region_24.30_spmd} | conditional | flops 3268552192 | bytes 122966848 | solution.py:113
  1113.5 247.6 %while.66 = (s32[]{:T(128)}, f32[8,128,128]{2,1,0:T(8,128)S(1)}, s32[64]{0:T(128)S(1)}, f32[8,64]{0,1:T(8,128)S(1)}, f32[8,64,128]{2,0,1:T(8,128)S(1)}, /*index=5*/s32[]{:T(128)}, s32[]{:T(128)}, s32[]{:T(128)}) while((s32[]{:T(128)}, f32[8,128,128]{2,1,0:T(8,128)S(1)}, s32[64]{0:T(128)S(1)}, f32[8,64]{0,1:T(8,128)S(1)}, ...), condition=%wide.region_27.27_spmd, body=%wide.region_26.26_spmd.sunk | while | flops 1836037 | bytes 1614071 | solution.py:31
  1363.3 4.1 convolution_bitcast_fusion.3
  1367.4 3.6 fusion.36
  1371.1 3.4 convert_reduce_fusion.3
  1374.5 8.4 fusion.37
  1385.0 265.6 %conditional.11 = ((f32[1024,8,128]{0,2,1:T(8,128)}, f32[8,1024]{1,0:T(8,128)S(1)}, f32[8,1024]{1,0:T(8,128)S(1)}, f32[1024,8,128]{2,0,1:T(8,128)})) conditional(s32[]{:T(128)} %bitcast.100, (f32[1024,8,128]{0,2,1:T(8,128)}, f32[8,1024]{1,0:T(8,128)S(1)}, f32[8,1024]{1,0:T(8,128)S(1)}, f32[1024,8,128]{2,0,1:T(8,128)}) %get-tuple-element.1204, ...), branch_computations={%region_30.31_spmd, %region_31.37_spmd} | conditional | flops 3268552192 | bytes 122966848 | solution.py:113
  1385.4 243.0 %while.67 = (s32[]{:T(128)}, f32[8,128,128]{2,1,0:T(8,128)S(1)}, s32[64]{0:T(128)S(1)}, f32[8,64]{0,1:T(8,128)S(1)}, f32[8,64,128]{2,0,1:T(8,128)S(1)}, /*index=5*/s32[]{:T(128)}, s32[]{:T(128)}, s32[]{:T(128)}) while((s32[]{:T(128)}, f32[8,128,128]{2,1,0:T(8,128)S(1)}, s32[64]{0:T(128)S(1)}, f32[8,64]{0,1:T(8,128)S(1)}, ...), condition=%wide.region_34.34_spmd, body=%wide.region_33.33_spmd.sunk | while | flops 1836037 | bytes 1614071 | solution.py:31
  1630.6 4.1 convolution_bitcast_fusion.4
  1636.8 3.1 convert_reduce_fusion.4
  1639.9 8.4 fusion.49
  1650.6 262.9 %conditional.12 = ((f32[1024,8,128]{0,2,1:T(8,128)}, f32[8,1024]{1,0:T(8,128)S(1)}, f32[8,1024]{1,0:T(8,128)S(1)}, f32[1024,8,128]{2,0,1:T(8,128)})) conditional(s32[]{:T(128)} %bitcast.99, (f32[1024,8,128]{0,2,1:T(8,128)}, f32[8,1024]{1,0:T(8,128)S(1)}, f32[8,1024]{1,0:T(8,128)S(1)}, f32[1024,8,128]{2,0,1:T(8,128)}) %get-tuple-element.1205, ...), branch_computations={%region_37.38_spmd, %region_38.44_spmd} | conditional | flops 3268552704 | bytes 106190752 | solution.py:113
  1653.6 234.8 %while.68 = (s32[]{:T(128)}, f32[8,128,128]{2,1,0:T(8,128)S(1)}, s32[64]{0:T(128)S(1)}, f32[8,64]{0,1:T(8,128)S(1)}, f32[8,64,128]{2,0,1:T(8,128)S(1)}, /*index=5*/s32[]{:T(128)}, s32[]{:T(128)}, s32[]{:T(128)}) while((s32[]{:T(128)}, f32[8,128,128]{2,1,0:T(8,128)S(1)}, s32[64]{0:T(128)S(1)}, f32[8,64]{0,1:T(8,128)S(1)}, ...), condition=%wide.region_41.41_spmd, body=%wide.region_40.40_spmd.sunk | while | flops 1836037 | bytes 1614071 | solution.py:31
  1890.5 5.3 convolution_bitcast_fusion.5
  1895.8 4.3 fusion.60
  1900.2 2.8 convert_reduce_fusion.5
  1903.1 8.4 fusion.61
  1913.6 284.2 %conditional.13 = (f32[8,1024]{1,0:T(8,128)S(1)}, f32[1024,8,128]{0,2,1:T(8,128)}) conditional(s32[]{:T(128)} %bitcast.98, (f32[8,1024]{1,0:T(8,128)S(1)}, f32[1024,8,128]{2,0,1:T(8,128)}) %tuple.84, (s32[]{:T(128)}, pred[384]{0:T(512)(128)(4,1)S(1)}, pred[384]{0:T(512)(128)(4,1)S(1)}, bf16[1,8,64,128]{3,1,2,0:T(8,128)(2,1)S(1)}, ...), branch_computations={%region_44.45_spmd, %region_45.51_spmd} | conditional | flops 3267495936 | bytes 85022576 | solution.py:113
  1914.1 256.9 %while.69 = (s32[]{:T(128)}, f32[8,128,128]{2,1,0:T(8,128)S(1)}, s32[64]{0:T(128)S(1)}, f32[8,64]{0,1:T(8,128)S(1)}, f32[8,64,128]{2,0,1:T(8,128)S(1)}, /*index=5*/s32[]{:T(128)}, s32[]{:T(128)}, s32[]{:T(128)}) while((s32[]{:T(128)}, f32[8,128,128]{2,1,0:T(8,128)S(1)}, s32[64]{0:T(128)S(1)}, f32[8,64]{0,1:T(8,128)S(1)}, ...), condition=%wide.region_48.48_spmd, body=%wide.region_47.47_spmd.sunk | while | flops 1836037 | bytes 1614071 | solution.py:31
  2171.0 8.5 fusion.103
  2181.5 2.8 convert_reduce_fusion.6
  2184.4 7.9 fusion.73
  2192.3 5.3 copy.150
  2197.9 2.8 divide_convert_fusion
  2200.7 14.6 convolution_convert_fusion
  2215.3 69.2 %reduce-scatter.2.cloned.1.call-done = bf16[1024,1024]{1,0:T(8,128)(2,1)} async-done(((bf16[1024,4096]{1,0:T(8,128)(2,1)}), bf16[1024,1024]{1,0:T(8,128)(2,1)}) %reduce-scatter.2.cloned.1.call-update) | async-done | bytes 2097168 | tf_op jit(solution)/shard_map/reduce_scatter | solution.py:121
  (3331 shorter events, 920.4 us)
Async XLA Ops:
  6.5 2277.9 %reduce-scatter.2.cloned.1.call-start = ((), (), s32[]{:S(2)}) async-start(), calls=%async_computation.1 | async-start | bytes 10485760 | tf_op jit(solution)/shard_map/reduce_scatter | solution.py:121
  6.5 24.6 %collective-permute-start = (bf16[384,1024]{1,0:T(8,128)(2,1)}, bf16[384,1024]{1,0:T(8,128)(2,1)S(1)}, u32[]{:S(2)}, u32[]{:S(2)}) collective-permute-start(bf16[384,1024]{1,0:T(8,128)(2,1)} %param.38), channel_id=1, source_target_pairs={{0,4},{4,8},{8,12},{12,16},{16,20},{20,24},{24,28},{28,0},{1,5},{5... | collective-permute-start | bytes 2359304 | tf_op jit(solution)/shard_map/ppermute | solution.py:12
  9.5 38.5 %collective-permute-start.1 = (bf16[384,1024]{1,0:T(8,128)(2,1)}, bf16[384,1024]{1,0:T(8,128)(2,1)S(1)}, u32[]{:S(2)}, u32[]{:S(2)}) collective-permute-start(bf16[384,1024]{1,0:T(8,128)(2,1)} %param.39), channel_id=1, source_target_pairs={{0,4},{4,8},{8,12},{12,16},{16,20},{20,24},{24,28},{28,0},{1,5},{5... | collective-permute-start | bytes 2359304 | tf_op jit(solution)/shard_map/ppermute | solution.py:12
  31.1 16.9 copy-start.23
  31.1 33.8 %collective-permute-start.4 = (bf16[384,1024]{1,0:T(8,128)(2,1)S(1)}, bf16[384,1024]{1,0:T(8,128)(2,1)}, u32[]{:S(2)}, u32[]{:S(2)}) collective-permute-start(bf16[384,1024]{1,0:T(8,128)(2,1)S(1)} %collective-permute-done), channel_id=1, source_target_pairs={{0,4},{4,8},{8,12},{12,16},{16,20},{20,24},{24,28},{28,0},{1,5},{5... | collective-permute-start | bytes 2359304 | tf_op jit(solution)/shard_map/ppermute | solution.py:12
  47.9 17.0 copy-start.30
  47.9 33.8 %collective-permute-start.5 = (bf16[384,1024]{1,0:T(8,128)(2,1)S(1)}, bf16[384,1024]{1,0:T(8,128)(2,1)}, u32[]{:S(2)}, u32[]{:S(2)}) collective-permute-start(bf16[384,1024]{1,0:T(8,128)(2,1)S(1)} %collective-permute-done.1), channel_id=1, source_target_pairs={{0,4},{4,8},{8,12},{12,16},{16,20},{20,24},{24,28},{28,0},{1,5},{5... | collective-permute-start | bytes 2359304 | tf_op jit(solution)/shard_map/ppermute | solution.py:12
  64.9 33.6 %collective-permute-start.8 = (bf16[384,1024]{1,0:T(8,128)(2,1)}, bf16[384,1024]{1,0:T(8,128)(2,1)S(1)}, u32[]{:S(2)}, u32[]{:S(2)}) collective-permute-start(bf16[384,1024]{1,0:T(8,128)(2,1)} %collective-permute-done.4), channel_id=1, source_target_pairs={{0,4},{4,8},{8,12},{12,16},{16,20},{20,24},{24,28},{28,0},{1,5},{5... | collective-permute-start | bytes 2359304 | tf_op jit(solution)/shard_map/ppermute | solution.py:12
  81.8 33.7 %collective-permute-start.9 = (bf16[384,1024]{1,0:T(8,128)(2,1)}, bf16[384,1024]{1,0:T(8,128)(2,1)}, u32[]{:S(2)}, u32[]{:S(2)}) collective-permute-start(bf16[384,1024]{1,0:T(8,128)(2,1)} %collective-permute-done.5), channel_id=1, source_target_pairs={{0,4},{4,8},{8,12},{12,16},{16,20},{20,24},{24,28},{28,0},{1,5},{5... | collective-permute-start | bytes 2359304 | tf_op jit(solution)/shard_map/ppermute | solution.py:12
  83.4 71.6 %collective-permute-start.2 = (bf16[1,8,64,128]{3,1,2,0:T(8,128)(2,1)}, bf16[1,8,64,128]{3,1,2,0:T(8,128)(2,1)S(1)}, u32[]{:S(2)}, u32[]{:S(2)}) collective-permute-start(bf16[1,8,64,128]{3,1,2,0:T(8,128)(2,1)} %copy.98), channel_id=1, source_target_pairs={{0,4},{4,8},{8,12},{12,16},{16,20},{20,24},{24,28},{28,0},{1,5},{5... | collective-permute-start | bytes 393224 | tf_op jit(solution)/shard_map/ppermute | solution.py:12
  85.6 175.3 %collective-permute-start.3 = (bf16[1,8,64]{1,2,0:T(8,128)(2,1)S(1)}, bf16[1,8,64]{1,2,0:T(8,128)(2,1)S(1)}, u32[]{:S(2)}, u32[]{:S(2)}) collective-permute-start(bf16[1,8,64]{1,2,0:T(8,128)(2,1)S(1)} %copy.99), channel_id=1, source_target_pairs={{0,4},{4,8},{8,12},{12,16},{16,20},{20,24},{24,28},{28,0},{1,5},{5... | collective-permute-start | bytes 3080 | tf_op jit(solution)/shard_map/ppermute | solution.py:12
  98.5 20.7 copy-start.21
  98.5 37.0 %collective-permute-start.12 = (bf16[384,1024]{1,0:T(8,128)(2,1)S(1)}, bf16[384,1024]{1,0:T(8,128)(2,1)}, u32[]{:S(2)}, u32[]{:S(2)}) collective-permute-start(bf16[384,1024]{1,0:T(8,128)(2,1)S(1)} %collective-permute-done.8), channel_id=1, source_target_pairs={{0,4},{4,8},{8,12},{12,16},{16,20},{20,24},{24,28},{28,0},{1,5},{5... | collective-permute-start | bytes 2359304 | tf_op jit(solution)/shard_map/ppermute | solution.py:12
  115.5 36.9 %collective-permute-start.13 = (bf16[384,1024]{1,0:T(8,128)(2,1)}, bf16[384,1024]{1,0:T(8,128)(2,1)}, u32[]{:S(2)}, u32[]{:S(2)}) collective-permute-start(bf16[384,1024]{1,0:T(8,128)(2,1)} %collective-permute-done.9), channel_id=1, source_target_pairs={{0,4},{4,8},{8,12},{12,16},{16,20},{20,24},{24,28},{28,0},{1,5},{5... | collective-permute-start | bytes 2359304 | tf_op jit(solution)/shard_map/ppermute | solution.py:12
  135.5 33.6 %collective-permute-start.16 = (bf16[384,1024]{1,0:T(8,128)(2,1)}, bf16[384,1024]{1,0:T(8,128)(2,1)S(1)}, u32[]{:S(2)}, u32[]{:S(2)}) collective-permute-start(bf16[384,1024]{1,0:T(8,128)(2,1)} %collective-permute-done.12), channel_id=1, source_target_pairs={{0,4},{4,8},{8,12},{12,16},{16,20},{20,24},{24,28},{28,0},{1,5},{5... | collective-permute-start | bytes 2359304 | tf_op jit(solution)/shard_map/ppermute | solution.py:12
  152.3 33.7 %collective-permute-start.17 = (bf16[384,1024]{1,0:T(8,128)(2,1)}, bf16[384,1024]{1,0:T(8,128)(2,1)}, u32[]{:S(2)}, u32[]{:S(2)}) collective-permute-start(bf16[384,1024]{1,0:T(8,128)(2,1)} %collective-permute-done.13), channel_id=1, source_target_pairs={{0,4},{4,8},{8,12},{12,16},{16,20},{20,24},{24,28},{28,0},{1,5},{5... | collective-permute-start | bytes 2359304 | tf_op jit(solution)/shard_map/ppermute | solution.py:12
  155.0 39.2 %copy-start.27 = (bf16[1,8,64,128]{3,1,2,0:T(8,128)(2,1)}, bf16[1,8,64,128]{3,1,2,0:T(8,128)(2,1)S(1)}, u32[]{:S(2)}) copy-start(bf16[1,8,64,128]{3,1,2,0:T(8,128)(2,1)S(1)} %collective-permute-done.2) | copy-start | bytes 393220
  155.0 39.2 %collective-permute-start.6 = (bf16[1,8,64,128]{3,1,2,0:T(8,128)(2,1)S(1)}, bf16[1,8,64,128]{3,1,2,0:T(8,128)(2,1)S(1)}, u32[]{:S(2)}, u32[]{:S(2)}) collective-permute-start(bf16[1,8,64,128]{3,1,2,0:T(8,128)(2,1)S(1)} %collective-permute-done.2), channel_id=1, source_target_pairs={{0,4},{4,8},{8,12},{12,16},{16,20},{20,24},{24,28},{28,0},{1,5},{5... | collective-permute-start | bytes 393224 | tf_op jit(solution)/shard_map/ppermute | solution.py:12
  169.1 25.1 %copy-start.19 = (bf16[384,1024]{1,0:T(8,128)(2,1)}, bf16[384,1024]{1,0:T(8,128)(2,1)S(1)}, u32[]{:S(2)}) copy-start(bf16[384,1024]{1,0:T(8,128)(2,1)S(1)} %collective-permute-done.16) | copy-start | bytes 2359300
  169.1 36.6 %collective-permute-start.20 = (bf16[384,1024]{1,0:T(8,128)(2,1)S(1)}, bf16[384,1024]{1,0:T(8,128)(2,1)}, u32[]{:S(2)}, u32[]{:S(2)}) collective-permute-start(bf16[384,1024]{1,0:T(8,128)(2,1)S(1)} %collective-permute-done.16), channel_id=1, source_target_pairs={{0,4},{4,8},{8,12},{12,16},{16,20},{20,24},{24,28},{28,0},{1,5},{5... | collective-permute-start | bytes 2359304 | tf_op jit(solution)/shard_map/ppermute | solution.py:12
  186.0 36.5 %collective-permute-start.21 = (bf16[384,1024]{1,0:T(8,128)(2,1)}, bf16[384,1024]{1,0:T(8,128)(2,1)}, u32[]{:S(2)}, u32[]{:S(2)}) collective-permute-start(bf16[384,1024]{1,0:T(8,128)(2,1)} %collective-permute-done.17), channel_id=1, source_target_pairs={{0,4},{4,8},{8,12},{12,16},{16,20},{20,24},{24,28},{28,0},{1,5},{5... | collective-permute-start | bytes 2359304 | tf_op jit(solution)/shard_map/ppermute | solution.py:12
  194.2 94.0 %copy-start.18 = (bf16[1,8,64,128]{3,2,1,0:T(8,128)(2,1)S(1)}, bf16[1,8,64,128]{3,2,1,0:T(8,128)(2,1)}, u32[]{:S(2)}) copy-start(bf16[1,8,64,128]{3,2,1,0:T(8,128)(2,1)} %param.40) | copy-start | bytes 393220
  194.2 94.0 %copy-start.29 = (bf16[1,8,64]{2,1,0:T(8,128)(2,1)S(1)}, bf16[1,8,64]{2,1,0:T(8,128)(2,1)}, u32[]{:S(2)}) copy-start(bf16[1,8,64]{2,1,0:T(8,128)(2,1)} %param.41) | copy-start | bytes 3076
  194.2 31.5 %copy-start.25 = (bf16[1,8,64,128]{3,1,2,0:T(8,128)(2,1)}, bf16[1,8,64,128]{3,1,2,0:T(8,128)(2,1)S(1)}, u32[]{:S(2)}) copy-start(bf16[1,8,64,128]{3,1,2,0:T(8,128)(2,1)S(1)} %collective-permute-done.6) | copy-start | bytes 393220
  194.2 31.5 %collective-permute-start.10 = (bf16[1,8,64,128]{3,1,2,0:T(8,128)(2,1)S(1)}, bf16[1,8,64,128]{3,1,2,0:T(8,128)(2,1)S(1)}, u32[]{:S(2)}, u32[]{:S(2)}) collective-permute-start(bf16[1,8,64,128]{3,1,2,0:T(8,128)(2,1)S(1)} %collective-permute-done.6), channel_id=1, source_target_pairs={{0,4},{4,8},{8,12},{12,16},{16,20},{20,24},{24,28},{28,0},{1,5},{5... | collective-permute-start | bytes 393224 | tf_op jit(solution)/shard_map/ppermute | solution.py:12
  205.7 1707.9 %collective-permute-start.24 = (bf16[384,1024]{1,0:T(8,128)(2,1)}, bf16[384,1024]{1,0:T(8,128)(2,1)S(1)}, u32[]{:S(2)}, u32[]{:S(2)}) collective-permute-start(bf16[384,1024]{1,0:T(8,128)(2,1)} %collective-permute-done.20), channel_id=1, source_target_pairs={{0,4},{4,8},{8,12},{12,16},{16,20},{20,24},{24,28},{28,0},{1,5},{5... | collective-permute-start | bytes 2359304 | tf_op jit(solution)/shard_map/ppermute | solution.py:12
  222.5 1691.1 %collective-permute-start.25 = (bf16[384,1024]{1,0:T(8,128)(2,1)}, bf16[384,1024]{1,0:T(8,128)(2,1)}, u32[]{:S(2)}, u32[]{:S(2)}) collective-permute-start(bf16[384,1024]{1,0:T(8,128)(2,1)} %collective-permute-done.21), channel_id=1, source_target_pairs={{0,4},{4,8},{8,12},{12,16},{16,20},{20,24},{24,28},{28,0},{1,5},{5... | collective-permute-start | bytes 2359304 | tf_op jit(solution)/shard_map/ppermute | solution.py:12
  225.7 35.2 %collective-permute-start.14 = (bf16[1,8,64,128]{3,1,2,0:T(8,128)(2,1)S(1)}, bf16[1,8,64,128]{3,1,2,0:T(8,128)(2,1)S(1)}, u32[]{:S(2)}, u32[]{:S(2)}) collective-permute-start(bf16[1,8,64,128]{3,1,2,0:T(8,128)(2,1)S(1)} %collective-permute-done.10), channel_id=1, source_target_pairs={{0,4},{4,8},{8,12},{12,16},{16,20},{20,24},{24,28},{28,0},{1,5},{5... | collective-permute-start | bytes 393224 | tf_op jit(solution)/shard_map/ppermute | solution.py:12
  260.9 7.8 collective-permute-start.18
  261.0 7.8 collective-permute-start.7
  268.8 6.4 collective-permute-start.11
  268.8 1644.8 %collective-permute-start.22 = (bf16[1,8,64,128]{3,1,2,0:T(8,128)(2,1)}, bf16[1,8,64,128]{3,1,2,0:T(8,128)(2,1)S(1)}, u32[]{:S(2)}, u32[]{:S(2)}) collective-permute-start(bf16[1,8,64,128]{3,1,2,0:T(8,128)(2,1)} %collective-permute-done.18), channel_id=1, source_target_pairs={{0,4},{4,8},{8,12},{12,16},{16,20},{20,24},{24,28},{28,0},{1,5},{5... | collective-permute-start | bytes 393224 | tf_op jit(solution)/shard_map/ppermute | solution.py:12
  275.2 6.4 collective-permute-start.15
  281.7 6.5 collective-permute-start.19
  288.2 1625.4 %collective-permute-start.23 = (bf16[1,8,64]{1,2,0:T(8,128)(2,1)}, bf16[1,8,64]{1,2,0:T(8,128)(2,1)S(1)}, u32[]{:S(2)}, u32[]{:S(2)}) collective-permute-start(bf16[1,8,64]{1,2,0:T(8,128)(2,1)} %collective-permute-done.19), channel_id=1, source_target_pairs={{0,4},{4,8},{8,12},{12,16},{16,20},{20,24},{24,28},{28,0},{1,5},{5... | collective-permute-start | bytes 3080 | tf_op jit(solution)/shard_map/ppermute | solution.py:12
  288.2 283.6 %copy-start.28 = (bf16[1,8,64,128]{3,1,2,0:T(8,128)(2,1)S(1)}, bf16[1,8,64,128]{3,1,2,0:T(8,128)(2,1)}, u32[]{:S(2)}) copy-start(bf16[1,8,64,128]{3,1,2,0:T(8,128)(2,1)} %copy-done.27) | copy-start | bytes 393220
  552.8 4.1 copy-start.24
  556.9 2.0 copy-start
  558.9 3.2 copy-start.5
  559.0 3.2 copy-start.31
  569.4 2.0 copy-start.6
  571.8 286.6 %copy-start.22 = (bf16[384,1024]{1,0:T(8,128)(2,1)S(1)}, bf16[384,1024]{1,0:T(8,128)(2,1)}, u32[]{:S(2)}) copy-start(bf16[384,1024]{1,0:T(8,128)(2,1)} %copy-done.21) | copy-start | bytes 2359300
  571.8 286.6 %copy-start.26 = (bf16[1,8,64,128]{3,1,2,0:T(8,128)(2,1)S(1)}, bf16[1,8,64,128]{3,1,2,0:T(8,128)(2,1)}, u32[]{:S(2)}) copy-start(bf16[1,8,64,128]{3,1,2,0:T(8,128)(2,1)} %copy-done.25) | copy-start | bytes 393220
  841.1 3.6 copy-start.1
  844.8 3.1 copy-start.7
  856.3 2.0 copy-start.8
  1097.3 2.0 copy-start.2
  1099.3 3.2 copy-start.9
  1110.9 2.0 copy-start.10
  1113.1 271.9 %copy-start.20 = (bf16[384,1024]{1,0:T(8,128)(2,1)S(1)}, bf16[384,1024]{1,0:T(8,128)(2,1)}, u32[]{:S(2)}) copy-start(bf16[384,1024]{1,0:T(8,128)(2,1)} %copy-done.19) | copy-start | bytes 2359300
  1367.4 3.6 copy-start.3
  1371.1 3.4 copy-start.11
  1382.9 2.0 copy-start.12
  1634.7 2.0 copy-start.4
  1636.8 3.1 copy-start.13
  1648.3 2.0 copy-start.14
  1900.2 2.9 copy-start.15
  1911.5 2.0 copy-start.16
  2181.5 2.9 copy-start.17
Sparse Core Ops, SparseCore 0:
  2215.4 68.9 reduce-scatter.1
where the time goes:
time: 2330 us; the launch traced here: 2290 us
  loops' own time  875 us (38%)
  matrix products  551 us (24%)
  local copies, waits for them, and re-layouts  327 us (14%)
  waiting for transfers between devices  314 us (13%)
  other arithmetic  197 us (8%)
    another operation x7, loops' own time, shard_product(): lax.scan(reflect_once, initial, jnp.arange(unit_rows.shape[1]))  872 us
    dot_general x448, matrix products, reflect_once(): jnp.einsum('hij,hj->hi', product, vector, precision=lax.Precision.HIGHEST)  414 us
    dynamic_slice x448, local copies, waits for them, and re-layouts, shard_product(): lax.scan(reflect_once, initial, jnp.arange(unit_rows.shape[1]))  280 us
    ppermute x26, waiting for transfers between devices, shifted(): return lax.ppermute(value, axis, pairs)  245 us
    sub x448, other arithmetic, reflect_once(): product - weight[:, None, None] * applied[:, :, None] * vector[:, None, :]  126 us
    reduce_scatter x1, waiting for transfers between devices, shards(): lax.psum_scatter(partial_terms.astype(jnp.bfloat16), 'head', scatter_dime...  69.2 us
    dot_general x8, matrix products, attend(): jnp.einsum('hrk,khd->rhd', weights, value_layout, preferred_element_type=...  65.2 us
  transfers between devices with their start and end apart: 27, of which 18 were waited for; matrix products, arithmetic and copies ran while one was open for 39% of the time, Pallas kernels for 0%

commit v1 on v0

v1 whole, which is shorter than its diff:
```python
import functools
import math

import jax
import jax.numpy as jnp
from jax import lax
from jax.experimental import pallas as pl
from jax.experimental.pallas import tpu as pltpu
from jax.sharding import PartitionSpec as P

NT = (((1,), (1,)), ((), ()))
NN = (((1,), (0,)), ((), ()))


def dot32(a, b, dims):
    return lax.dot_general(a, b, dims, preferred_element_type=jnp.float32)


def dot_exact(a, b, dims):
    return lax.dot_general(
        a, b, dims, precision=lax.Precision.HIGHEST, preferred_element_type=jnp.float32
    )


def halves(x):
    high = x.astype(jnp.bfloat16)
    low = (x - high.astype(jnp.float32)).astype(jnp.bfloat16)
    return high, low


def factor_kernel(rank, unit, r_ref, b_ref, w_ref):
    row = lax.broadcasted_iota(jnp.int32, (unit, unit), 0)
    col = lax.broadcasted_iota(jnp.int32, (unit, unit), 1)
    apart = row ^ col
    upper = row < col
    eye = jnp.where(apart == 0, 1.0, 0.0)
    for start in range(0, r_ref.shape[0], unit):
        raw = r_ref[start : start + unit, :].astype(jnp.float32)
        beta = b_ref[start : start + unit, :]
        inverse = 1.0 / jnp.sqrt(jnp.sum(raw * raw, axis=-1, keepdims=True) + 1e-06)
        vectors = raw * inverse
        gram = dot_exact(vectors, vectors, NT)
        coupling = jnp.where(upper & (apart < rank), beta * gram, 0.0)
        solved = eye - jnp.where(apart == 1, coupling, 0.0)
        size = 2
        while size < rank:
            between = jnp.where((apart >= size) & (apart < 2 * size), coupling, 0.0)
            solved = solved - dot_exact(solved, dot_exact(between, solved, NN), NN)
            size *= 2
        w_ref[start : start + unit, :] = inverse * dot_exact(solved, beta * vectors, NN)


def attend_kernel(n, blocks, scal_ref, q_ref, kv_ref, r_ref, w_ref, o_ref, acc_ref, top_ref):
    rows, width = q_ref.shape
    keys = kv_ref.shape[2]
    block = rows // blocks
    rate = math.log2(math.e) / math.sqrt(width)
    me = scal_ref[0]
    length = scal_ref[1]
    live = scal_ref[2]
    ones = jnp.ones((keys, width), jnp.bfloat16)

    def attend(m, turn, mode):
        shard = lax.rem(me - m + n, n)
        shard_keys = kv_ref[shard, 0]
        if turn is not None:
            high, low = halves(turn)
            shard_keys = (dot32(shard_keys, high, NT) + dot32(shard_keys, low, NT)).astype(
                jnp.bfloat16
            )
        extended = jnp.concatenate([kv_ref[shard, 1], ones], axis=1)
        for b in range(blocks):
            here = slice(b * block, (b + 1) * block)
            scores = dot32(q_ref[here, :], shard_keys, NT)
            if mode == 0:
                position = scal_ref[3 + b] + lax.broadcasted_iota(jnp.int32, scores.shape, 0)
                key = lax.broadcasted_iota(jnp.int32, scores.shape, 1)
                scores = jnp.where(key <= position, scores, -jnp.inf)
            if mode == 2:
                key = lax.broadcasted_iota(jnp.int32, scores.shape, 1)
                scores = jnp.where(key >= keys - live, scores, -jnp.inf)
            top = jnp.max(scores, axis=-1, keepdims=True)
            if mode != 0:
                before = top_ref[here, :]
                top = jnp.maximum(top, before)
            weights = jnp.exp2((scores - top) * rate).astype(jnp.bfloat16)
            part = dot32(weights, extended, NN)
            if mode != 0:
                part = part + acc_ref[here, :] * jnp.exp2((before - top) * rate)
            if mode == 2:
                o_ref[here, :] = (part[:, :width] / part[:, width:]).astype(o_ref.dtype)
            else:
                acc_ref[here, :] = part
                top_ref[here, :] = top

    def advance(m, turn):
        shard = lax.rem(me - m + 1 + n, n)
        vectors = r_ref[shard, 0]
        high, low = halves(turn)
        ahigh, alow = halves(dot32(high, vectors, NT) + dot32(low, vectors, NT))
        whigh, wlow = halves(w_ref[shard, 0])
        return turn - (
            dot32(ahigh, whigh, NN) + (dot32(alow, whigh, NN) + dot32(ahigh, wlow, NN))
        )

    row = lax.broadcasted_iota(jnp.int32, (width, width), 0)
    col = lax.broadcasted_iota(jnp.int32, (width, width), 1)
    eye = jnp.where(row == col, 1.0, 0.0).astype(jnp.float32)
    attend(0, None, 0)

    def step(m, turn):
        turn = advance(m, turn)
        attend(m, turn, 1)
        return turn

    turn = lax.fori_loop(1, length - 1, step, eye)
    attend(length - 1, advance(length - 1, turn), 2)


def shards(queries, cache_keys, cache_values, reflect, betas, chain_len, block_start, live_len, w_out):
    rows = queries.shape[0]
    heads, rank, width = reflect.shape[1:]
    keys = cache_keys.shape[0]
    blocks = block_start.shape[1]
    n = lax.axis_size("ctx")
    groups = lax.axis_size("head")
    me = lax.axis_index("ctx")
    group = lax.axis_index("head")
    chunks = 4
    per = heads // chunks
    columns = w_out.shape[1] // groups

    per_unit = max(1, min(heads, 256 // rank))
    factors = pl.pallas_call(
        functools.partial(factor_kernel, rank, per_unit * rank),
        out_shape=jax.ShapeDtypeStruct((heads * rank, width), jnp.float32),
        compiler_params=pltpu.CompilerParams(vmem_limit_bytes=40 * 2**20),
        name="factors",
    )(
        reflect[0].reshape(heads * rank, width),
        betas[0].astype(jnp.float32).reshape(heads * rank, 1),
    )
    all_reflect = lax.all_gather(reflect[0], "ctx")
    all_factors = lax.all_gather(factors.reshape(heads, rank, width), "ctx")
    gathered = []
    for chunk in range(chunks):
        cut = slice(chunk * per * width, (chunk + 1) * per * width)
        gathered.append(lax.all_gather(jnp.stack([cache_keys[:, cut], cache_values[:, cut]]), "ctx"))

    pieces = [lax.dynamic_slice_in_dim(w_out, group * columns, columns, 1)]
    for shift in range(1, groups):
        piece = lax.dynamic_slice_in_dim(
            w_out, lax.rem(group + shift, groups) * columns, columns, 1
        )
        pieces.append(
            lax.ppermute(piece, "head", [(i, (i + shift) % groups) for i in range(groups)])
        )
    stack = jnp.stack(pieces)

    scalars = jnp.concatenate(
        [me.astype(jnp.int32)[None], chain_len, live_len, block_start[0]]
    )
    outcome = None
    for chunk in range(chunks):
        base = chunk * per
        attended = pl.pallas_call(
            functools.partial(attend_kernel, n, blocks),
            out_shape=jax.ShapeDtypeStruct((rows, per * width), jnp.bfloat16),
            grid_spec=pltpu.PrefetchScalarGridSpec(
                num_scalar_prefetch=1,
                grid=(per,),
                in_specs=[
                    pl.BlockSpec((rows, width), lambda h, s, base=base: (0, base + h)),
                    pl.BlockSpec((n, 2, keys, width), lambda h, s: (0, 0, 0, h)),
                    pl.BlockSpec((n, 1, rank, width), lambda h, s, base=base: (0, base + h, 0, 0)),
                    pl.BlockSpec((n, 1, rank, width), lambda h, s, base=base: (0, base + h, 0, 0)),
                ],
                out_specs=pl.BlockSpec((rows, width), lambda h, s: (0, h)),
                scratch_shapes=[
                    pltpu.VMEM((rows, 2 * width), jnp.float32),
                    pltpu.VMEM((rows, 1), jnp.float32),
                ],
            ),
            compiler_params=pltpu.CompilerParams(vmem_limit_bytes=40 * 2**20),
            cost_estimate=pl.CostEstimate(
                flops=per * 16 * rows * keys * width * 2,
                bytes_accessed=per * (16 * keys * width * 2 + 4 * rows * width),
                transcendentals=per * 8 * rows * keys,
            ),
            name="attend",
        )(scalars, queries, gathered[chunk], all_reflect, all_factors)
        shared = lax.all_gather(attended, "head", axis=1, tiled=True)
        share = jnp.concatenate(
            [
                lax.dynamic_slice(
                    stack,
                    (lax.rem(group - g + groups, groups), base * width, 0),
                    (1, per * width, columns),
                )[0]
                for g in range(groups)
            ]
        )
        term = jnp.dot(shared, share, preferred_element_type=jnp.float32)
        outcome = term if outcome is None else outcome + term
    return outcome.astype(jnp.bfloat16)


def solution(mesh):
    return jax.shard_map(
        shards,
        mesh=mesh,
        in_specs=(
            P("ctx", "head"),
            P("ctx", "head"),
            P("ctx", "head"),
            P("ctx", "head", None, None),
            P("ctx", "head", None),
            P("ctx"),
            P("ctx", None),
            P("ctx"),
            P("head", None),
        ),
        out_specs=P("ctx", "head"),
        check_vma=False,
    )
```

time: 2330 us -> 497 us (0.21); the launches traced: 2290 us -> 493 us
  loops' own time: 875 us -> 0 us
  matrix products: 551 us -> 27.6 us
  local copies, waits for them, and re-layouts: 327 us -> 28.1 us
  other arithmetic: 197 us -> 7.68 us
  Pallas kernels: 0 us -> 125 us
  waiting for transfers between devices: 314 us -> 287 us
    another operation x14 -> x0, loops' own time: 875 us -> none  [the longest x7 872 us: shard_product(): lax.scan(reflect_once, initial, jnp.arange(unit_rows.shape[1]))]
    dot_general x472 -> x4, matrix products: 551 us -> 27.6 us  [shards(): term = jnp.dot(shared, share, preferred_element_type=jnp.float32)]
    dynamic_slice x896 -> x0, local copies, waits for them, and re-layouts: 285 us -> none  [the longest x448 280 us: shard_product(): lax.scan(reflect_once, initial, jnp.arange(unit_rows.shape[1]))]
    all_gather x0 -> x10, waiting for transfers between devices: none -> 214 us  [the longest x4 140 us: shards(): lax.all_gather(jnp.stack([cache_keys[:, cut], cache_values[:, cut]]), 'ctx')]
    ppermute x26 -> x3, waiting for transfers between devices: 245 us -> 72.3 us  [shards(): lax.ppermute(piece, 'head', [(i, (i + shift) % groups) for i in range(gro...]
    sub x448 -> x0, other arithmetic: 126 us -> none  [reflect_once(): product - weight[:, None, None] * applied[:, :, None] * vector[:, None, :]]
    pallas_call x0 -> x5, Pallas kernels: none -> 125 us  [the longest x4 112 us: shards(): pl.pallas_call(functools.partial(attend_kernel, n, blocks), out_shape=jax...]
    reduce_scatter x1 -> x0, waiting for transfers between devices: 69.2 us -> none  [shards(): lax.psum_scatter(partial_terms.astype(jnp.bfloat16), 'head', scatter_dime...]
  transfers between devices with their start and end apart: 27 -> 13, of which waited for: 18 -> 9; matrix products, arithmetic and copies ran while one was open for 39% -> 8% of each run, Pallas kernels for 0% -> 25%
where the time goes in v1:
time: 497 us; the launch traced here: 493 us
  waiting for transfers between devices  287 us (58%)
  Pallas kernels  125 us (25%)
  local copies, waits for them, and re-layouts  28.1 us (6%)
  matrix products  27.6 us (6%)
  between operations  14.9 us (3%)
  other arithmetic  7.68 us (2%)
    all_gather x4, waiting for transfers between devices, shards(): lax.all_gather(jnp.stack([cache_keys[:, cut], cache_values[:, cut]]), 'ctx')  140 us
    pallas_call x4, Pallas kernels, shards(): pl.pallas_call(functools.partial(attend_kernel, n, blocks), out_shape=jax...  112 us
    ppermute x3, waiting for transfers between devices, shards(): lax.ppermute(piece, 'head', [(i, (i + shift) % groups) for i in range(gro...  72.3 us
    all_gather x1, waiting for transfers between devices, shards(): all_factors = lax.all_gather(factors.reshape(heads, rank, width), 'ctx')  50.2 us
    dot_general x4, matrix products, shards(): term = jnp.dot(shared, share, preferred_element_type=jnp.float32)  27.6 us
    all_gather x1, waiting for transfers between devices, shards(): all_reflect = lax.all_gather(reflect[0], 'ctx')  23.8 us
    unnamed x26, local copies, waits for them, and re-layouts  16.1 us
    pallas_call x1, Pallas kernels, shards(): pl.pallas_call(functools.partial(factor_kernel, rank, per_unit * rank), o...  12.9 us
  transfers between devices with their start and end apart: 13, of which 9 were waited for; matrix products, arithmetic and copies ran while one was open for 8% of the time, Pallas kernels for 25%

profile of v1, /device:TPU:0, one launch (start us, length us, event | category | flops | bytes accessed | tf_op | source)
XLA Modules:
  0.0 492.6 jit_solution(10791622982093154584)
XLA Ops:
  6.5 0.0 all-gather.15.cloned.1.call-start
  6.5 0.7 all-gather.15.cloned.1.call-update
  7.3 0.0 all-gather.17.cloned.1.call-start
  7.3 0.9 reshape.18.b_ref
  8.2 0.0 copy-start
  8.2 0.9 copy-done
  9.1 12.9 %factors.1 = f32[512,128]{1,0:T(8,128)} custom-call(bf16[512,128]{1,0:T(8,128)(2,1)S(1)} %bitcast.65, f32[512,1]{1,0:T(8,128)S(1)} %reshape.18.b_ref), custom_call_target="tpu_custom_call" | custom-call | tf_op jit(solution)/shard_map/factors/pallas_call | solution.py:134
  22.0 0.0 all-gather.17.cloned.1.call-update
  22.0 0.0 all-gather.29.cloned.1.call-start
  22.1 1.6 slice_bitcast_fusion
  23.7 0.8 pad_maximum_fusion.2
  24.5 0.0 all-gather.29.cloned.1.call-update
  24.5 0.0 all-gather.27.cloned.1.call-start
  24.5 0.8 pad_maximum_fusion.1
  25.3 0.0 all-gather.27.cloned.1.call-update
  25.3 0.0 all-gather.31.cloned.1.call-start
  25.4 0.8 pad_maximum_fusion.3
  26.2 0.0 all-gather.31.cloned.1.call-update
  26.2 0.0 all-gather.33.cloned.1.call-start
  26.3 0.8 pad_maximum_fusion.4
  27.0 0.0 all-gather.33.cloned.1.call-update
  27.1 0.2 all-gather.21.cloned.1.call-start
  28.6 0.0 copy-done.12
  28.6 0.1 pad_add_fusion.scal_ref
  28.7 23.8 %all-gather.15.cloned.1.call-done.r_ref = bf16[8,8,64,128]{3,2,1,0:T(8,128)(2,1)} async-done(((bf16[1,8,64,128]{3,2,1,0:T(8,128)(2,1)}), bf16[8,8,64,128]{3,2,1,0:T(8,128)(2,1)}) %all-gather.15.cloned.1.call-update) | async-done | bytes 1048592 | tf_op jit(solution)/shard_map/all_gather | solution.py:143
  52.4 50.2 %all-gather.17.cloned.1.call-done.w_ref = f32[8,8,64,128]{3,2,1,0:T(8,128)} async-done(((f32[1,8,64,128]{3,2,1,0:T(8,128)}), f32[8,8,64,128]{3,2,1,0:T(8,128)}) %all-gather.17.cloned.1.call-update) | async-done | bytes 2097168 | tf_op jit(solution)/shard_map/all_gather | solution.py:144
  102.6 61.2 %all-gather.29.cloned.1.call-done = bf16[16,384,256]{2,1,0:T(8,128)(2,1)} async-done(((bf16[2,384,256]{2,1,0:T(8,128)(2,1)}), bf16[16,384,256]{2,1,0:T(8,128)(2,1)}) %all-gather.29.cloned.1.call-update) | async-done | bytes 3145744 | tf_op jit(solution)/shard_map/all_gather | solution.py:148
  163.8 0.0 copy-done.5
  163.8 1.9 copy-done.4
  165.7 1.6 copy-done.6
  167.3 1.2 copy-done.10
  168.5 28.0 %attend.5 = bf16[1024,256]{1,0:T(8,128)(2,1)} custom-call(s32[7]{0:T(128)S(1)} %pad_add_fusion.scal_ref, bf16[1024,1024]{1,0:T(8,128)(2,1)S(1)} %copy-done.5, bf16[8,2,384,256]{3,2,1,0:T(8,128)(2,1)S(1)} %bitcast.69, bf16[8,8,64,128]{3,2,1,0:T(8,128)(2,1)S(1)} %copy-done.10, f32[8,8,64,128]{3,2,1,0:T(8,128)S(1)} %copy-done.6), custom_call_target="tpu_custom_call" | custom-call | flops 3221225472 | bytes 4194304 | tf_op jit(solution)/shard_map/attend/pallas_call | solution.py:166
  196.5 0.0 all-gather.21.cloned.1.call-update
  196.6 0.0 all-gather.19.cloned.1.call-start
  196.6 28.3 %all-gather.27.cloned.1.call-done = bf16[16,384,256]{2,1,0:T(8,128)(2,1)} async-done(((bf16[2,384,256]{2,1,0:T(8,128)(2,1)}), bf16[16,384,256]{2,1,0:T(8,128)(2,1)}) %all-gather.27.cloned.1.call-update) | async-done | bytes 3145744 | tf_op jit(solution)/shard_map/all_gather | solution.py:148
  224.9 1.9 copy-done.3
  226.8 1.6 copy-done.7
  228.4 28.0 %attend.4 = bf16[1024,256]{1,0:T(8,128)(2,1)} custom-call(s32[7]{0:T(128)S(1)} %pad_add_fusion.scal_ref, bf16[1024,1024]{1,0:T(8,128)(2,1)S(1)} %copy-done.5, bf16[8,2,384,256]{3,2,1,0:T(8,128)(2,1)S(1)} %bitcast.68, bf16[8,8,64,128]{3,2,1,0:T(8,128)(2,1)S(1)} %copy-done.11, f32[8,8,64,128]{3,2,1,0:T(8,128)S(1)} %copy-done.7), custom_call_target="tpu_custom_call" | custom-call | flops 3221225472 | bytes 4194304 | tf_op jit(solution)/shard_map/attend/pallas_call | solution.py:166
  256.4 0.0 all-gather.19.cloned.1.call-update
  256.4 0.0 all-gather.23.cloned.1.call-start
  256.4 29.8 %all-gather.31.cloned.1.call-done = bf16[16,384,256]{2,1,0:T(8,128)(2,1)} async-done(((bf16[2,384,256]{2,1,0:T(8,128)(2,1)}), bf16[16,384,256]{2,1,0:T(8,128)(2,1)}) %all-gather.31.cloned.1.call-update) | async-done | bytes 3145744 | tf_op jit(solution)/shard_map/all_gather | solution.py:148
  286.3 1.9 copy-done.2
  288.2 1.6 copy-done.8
  289.8 28.0 %attend.6 = bf16[1024,256]{1,0:T(8,128)(2,1)} custom-call(s32[7]{0:T(128)S(1)} %pad_add_fusion.scal_ref, bf16[1024,1024]{1,0:T(8,128)(2,1)S(1)} %copy-done.5, bf16[8,2,384,256]{3,2,1,0:T(8,128)(2,1)S(1)} %bitcast.67, bf16[8,8,64,128]{3,2,1,0:T(8,128)(2,1)S(1)} %copy-done.11, f32[8,8,64,128]{3,2,1,0:T(8,128)S(1)} %copy-done.8), custom_call_target="tpu_custom_call" | custom-call | flops 3221225472 | bytes 4194304 | tf_op jit(solution)/shard_map/attend/pallas_call | solution.py:166
  317.8 0.0 all-gather.23.cloned.1.call-update
  317.8 0.0 all-gather.25.cloned.1.call-start
  317.9 7.0 %dynamic-slice_bitcast_fusion = (bf16[1,1024,1024]{2,1,0:T(8,128)(2,1)}, bf16[1024,1024]{1,0:T(8,128)(2,1)}, bf16[1024,1024]{1,0:T(8,128)(2,1)}, bf16[1024,1024]{1,0:T(8,128)(2,1)}) fusion(bf16[1024,4096]{1,0:T(8,128)(2,1)} %param.17, s32[]{:T(128)S(6)} %select_n.16, s32[]{:T(128)S(6)} %select_n.17, s32[]{:T(128)S(6)} %select_n.19, s32[]{:T(128)S(6)} %select_n.18), kind=kLoop, calls=%fused_computation.34 | loop fusion | bytes 16777232 | tf_op jit(solution)/shard_map/stack | solution.py:158
  324.9 0.2 collective-permute-start.2
  325.1 0.3 collective-permute-start
  325.4 1.5 collective-permute-start.1
  326.8 20.6 %all-gather.33.cloned.1.call-done = bf16[16,384,256]{2,1,0:T(8,128)(2,1)} async-done(((bf16[2,384,256]{2,1,0:T(8,128)(2,1)}), bf16[16,384,256]{2,1,0:T(8,128)(2,1)}) %all-gather.33.cloned.1.call-update) | async-done | bytes 3145744 | tf_op jit(solution)/shard_map/all_gather | solution.py:148
  347.4 1.9 copy-done.1
  349.3 1.6 copy-done.9
  350.9 28.0 %attend.7 = bf16[1024,256]{1,0:T(8,128)(2,1)} custom-call(s32[7]{0:T(128)S(1)} %pad_add_fusion.scal_ref, bf16[1024,1024]{1,0:T(8,128)(2,1)S(1)} %copy-done.5, bf16[8,2,384,256]{3,2,1,0:T(8,128)(2,1)S(1)} %bitcast.66, bf16[8,8,64,128]{3,2,1,0:T(8,128)(2,1)S(1)} %copy-done.11, f32[8,8,64,128]{3,2,1,0:T(8,128)S(1)} %copy-done.9), custom_call_target="tpu_custom_call" | custom-call | flops 3221225472 | bytes 4194304 | tf_op jit(solution)/shard_map/attend/pallas_call | solution.py:166
  378.9 0.0 all-gather.25.cloned.1.call-update
  378.9 3.1 collective-permute-done.2
  382.1 2.5 collective-permute-done
  384.6 66.6 %collective-permute-done.1 = bf16[1024,1024]{1,0:T(8,128)(2,1)} collective-permute-done((bf16[1024,1024]{1,0:T(8,128)(2,1)}, bf16[1024,1024]{1,0:T(8,128)(2,1)}, u32[]{:S(2)}, u32[]{:S(2)}) %collective-permute-start.1) | collective-permute-done | bytes 2097184 | tf_op jit(solution)/shard_map/ppermute | solution.py:156
  451.2 4.5 pad_maximum_fusion
  455.7 2.6 dynamic-slice_bitcast_fusion.4
  458.2 6.7 %fusion.8 = f32[1024,1024]{1,0:T(8,128)} fusion(bf16[1024,1024]{1,0:T(8,128)(2,1)} %all-gather.21.cloned.1.call-done, bf16[256,1024]{1,0:T(8,128)(2,1)} %get-tuple-element.13, bf16[256,1024]{1,0:T(8,128)(2,1)} %get-tuple-element.14, bf16[256,1024]{1,0:T(8,128)(2,1)} %get-tuple-element.15, bf16[256,1024]{1,0:T(8,128)(2,1)} %get-tuple-element.16), kind=kOutput, calls=%fused_computation.10 | convolution fusion | flops 2155872256 | bytes 8388608 | tf_op jit(solution)/shard_map/dot_general | solution.py:203
  464.9 6.5 %fusion = f32[1024,1024]{1,0:T(8,128)} fusion(bf16[1024,1024]{1,0:T(8,128)(2,1)} %all-gather.19.cloned.1.call-done, bf16[256,1024]{1,0:T(8,128)(2,1)} %get-tuple-element.17, bf16[256,1024]{1,0:T(8,128)(2,1)} %get-tuple-element.18, bf16[256,1024]{1,0:T(8,128)(2,1)} %get-tuple-element.19, bf16[256,1024]{1,0:T(8,128)(2,1)} %get-tuple-element.20), kind=kOutput, calls=%fused_computation.2 | convolution fusion | flops 2155872256 | bytes 8388608 | tf_op jit(solution)/shard_map/dot_general | solution.py:203
  471.4 6.2 %fusion.16 = f32[1024,1024]{1,0:T(8,128)} fusion(bf16[1024,1024]{1,0:T(8,128)(2,1)} %all-gather.23.cloned.1.call-done, bf16[256,1024]{1,0:T(8,128)(2,1)S(1)} %get-tuple-element.9, bf16[256,1024]{1,0:T(8,128)(2,1)S(1)} %get-tuple-element.10, bf16[256,1024]{1,0:T(8,128)(2,1)} %get-tuple-element.11, bf16[256,1024]{1,0:T(8,128)(2,1)} %get-tuple-element.12), kind=kOutput, calls=%fused_computation.18 | convolution fusion | flops 2155872256 | bytes 8388608 | tf_op jit(solution)/shard_map/dot_general | solution.py:203
  477.6 8.2 %add_convert_fusion = bf16[1024,1024]{1,0:T(8,128)(2,1)} fusion(f32[1024,1024]{1,0:T(8,128)} %fusion.16, f32[1024,1024]{1,0:T(8,128)} %fusion, f32[1024,1024]{1,0:T(8,128)} %fusion.8, bf16[1024,1024]{1,0:T(8,128)(2,1)} %all-gather.25.cloned.1.call-done, bf16[256,1024]{1,0:T(8,128)(2,1)S(1)} %get-tuple-element.6, bf16[256,1024]{1,0:T(8,128)(2,1)S(1)} %get-tuple-element.7, ...), kind=kOutput, calls=%fused_computation.1 | convolution fusion | flops 2160066560 | bytes 18874368 | tf_op jit(solution)/shard_map/dot_general | solution.py:203
  (17 shorter events, 0.0 us)
Async XLA Ops:
  6.5 45.9 %all-gather.15.cloned.1.call-start = ((), (), s32[]{:S(2)}) async-start(), calls=%async_computation | async-start | bytes 1179648 | tf_op jit(solution)/shard_map/all_gather | solution.py:143
  7.3 95.4 %all-gather.17.cloned.1.call-start = ((), (), s32[]{:S(2)}) async-start(), calls=%async_computation.1 | async-start | bytes 2359296 | tf_op jit(solution)/shard_map/all_gather | solution.py:144
  8.2 0.9 copy-start
  22.0 141.8 %all-gather.29.cloned.1.call-start = ((), (), s32[]{:S(2)}) async-start(), calls=%async_computation.7 | async-start | bytes 3538944 | tf_op jit(solution)/shard_map/all_gather | solution.py:148
  24.5 4.1 copy-start.12
  24.5 139.3 %copy-start.5 = (bf16[1024,1024]{1,0:T(8,128)(2,1)S(1)}, bf16[1024,1024]{1,0:T(8,128)(2,1)}, u32[]{:S(2)}) copy-start(bf16[1024,1024]{1,0:T(8,128)(2,1)} %q_ref.7) | copy-start | bytes 6291460
  24.5 200.4 %all-gather.27.cloned.1.call-start = ((), (), s32[]{:S(2)}) async-start(), calls=%async_computation.6 | async-start | bytes 3538944 | tf_op jit(solution)/shard_map/all_gather | solution.py:148
  25.3 260.9 %all-gather.31.cloned.1.call-start = ((), (), s32[]{:S(2)}) async-start(), calls=%async_computation.8 | async-start | bytes 3538944 | tf_op jit(solution)/shard_map/all_gather | solution.py:148
  26.2 321.2 %all-gather.33.cloned.1.call-start = ((), (), s32[]{:S(2)}) async-start(), calls=%async_computation.9 | async-start | bytes 3538944 | tf_op jit(solution)/shard_map/all_gather | solution.py:148
  27.1 431.2 %all-gather.21.cloned.1.call-start = ((), (), s32[]{:S(2)}) async-start(), calls=%async_computation.3 | async-start | bytes 2621440 | tf_op jit(solution)/shard_map/all_gather | solution.py:192
  163.8 1.9 copy-start.4
  165.7 1.6 copy-start.6
  167.3 1.2 copy-start.10
  168.5 56.4 %copy-start.11 = (bf16[8,8,64,128]{3,2,1,0:T(8,128)(2,1)S(1)}, bf16[8,8,64,128]{3,2,1,0:T(8,128)(2,1)}, u32[]{:S(2)}) copy-start(bf16[8,8,64,128]{3,2,1,0:T(8,128)(2,1)} %all-gather.15.cloned.1.call-done.r_ref) | copy-start | bytes 3145732
  196.6 268.4 %all-gather.19.cloned.1.call-start = ((), (), s32[]{:S(2)}) async-start(), calls=%async_computation.2 | async-start | bytes 2621440 | tf_op jit(solution)/shard_map/all_gather | solution.py:192
  224.9 1.9 copy-start.3
  226.8 1.6 copy-start.7
  256.4 215.0 %all-gather.23.cloned.1.call-start = ((), (), s32[]{:S(2)}) async-start(), calls=%async_computation.4 | async-start | bytes 2621440 | tf_op jit(solution)/shard_map/all_gather | solution.py:192
  286.3 1.9 copy-start.2
  288.2 1.6 copy-start.8
  317.8 159.8 %all-gather.25.cloned.1.call-start = ((), (), s32[]{:S(2)}) async-start(), calls=%async_computation.5 | async-start | bytes 2621440 | tf_op jit(solution)/shard_map/all_gather | solution.py:192
  324.9 57.2 %collective-permute-start.2 = (bf16[1024,1024]{1,0:T(8,128)(2,1)}, bf16[1024,1024]{1,0:T(8,128)(2,1)}, u32[]{:S(2)}, u32[]{:S(2)}) collective-permute-start(bf16[1024,1024]{1,0:T(8,128)(2,1)} %get-tuple-element.23), channel_id=1, source_target_pairs={{0,3},{1,0},{2,1},{3,2},{4,7},{5,4},{6,5},{7,6},{8,11},{9,8},{10,9... | collective-permute-start | bytes 6291464 | tf_op jit(solution)/shard_map/ppermute | solution.py:156
  325.1 59.5 %collective-permute-start = (bf16[1024,1024]{1,0:T(8,128)(2,1)}, bf16[1024,1024]{1,0:T(8,128)(2,1)}, u32[]{:S(2)}, u32[]{:S(2)}) collective-permute-start(bf16[1024,1024]{1,0:T(8,128)(2,1)} %get-tuple-element.22), channel_id=1, source_target_pairs={{0,1},{1,2},{2,3},{3,0},{4,5},{5,6},{6,7},{7,4},{8,9},{9,10},{10,1... | collective-permute-start | bytes 6291464 | tf_op jit(solution)/shard_map/ppermute | solution.py:156
  325.4 125.8 %collective-permute-start.1 = (bf16[1024,1024]{1,0:T(8,128)(2,1)}, bf16[1024,1024]{1,0:T(8,128)(2,1)}, u32[]{:S(2)}, u32[]{:S(2)}) collective-permute-start(bf16[1024,1024]{1,0:T(8,128)(2,1)} %get-tuple-element.24), channel_id=1, source_target_pairs={{0,2},{1,3},{2,0},{3,1},{4,6},{5,7},{6,4},{7,5},{8,10},{9,11},{10,... | collective-permute-start | bytes 6291464 | tf_op jit(solution)/shard_map/ppermute | solution.py:156
  347.4 1.9 copy-start.1
  349.3 1.6 copy-start.9
Sparse Core Ops, SparseCore 0:
  9.5 42.9 all-gather.14
  54.6 48.0 all-gather.16
  104.8 58.9 all-gather.28
  165.8 59.0 all-gather.26
  226.9 59.3 all-gather.30
  288.3 59.0 all-gather.32
  349.0 32.8 all-gather.20
  383.4 34.3 all-gather.18
  419.4 34.0 all-gather.22
  454.8 22.0 all-gather.24
